TPU v7x, 32 devices: a whole 2x2x4 slice. The times are simulated.
32 devices in a mesh: dom: 32 (over z, y, x, core).
Axes of the slice: x: 2, y: 2, z: 4, core: 2. Of those that a mesh axis runs over, the one named last changes fastest.
Arguments:
- positions: float32 [32, 3, 2048], P('dom'), may hold values from -6 to 6
- states: float32 [32, 5, 27, 256], P('dom'), may hold values from -6 to 6
- conn: int32 [32, 27, 256], P('dom'), may hold values from 0 to 2047
- send_nodes: int32 [32, 4, 32], P('dom'), may hold values from 0 to 2047
- recv_nodes: int32 [32, 4, 32], P('dom'), may hold values from 0 to 2047
- send_elems: int32 [32, 4, 16], P('dom'), may hold values from 0 to 255
- neighbours: int32 [32, 6, 256], P('dom'), may hold values from 0 to 319
- live: int32 [32], P('dom'), may hold values from 128 to 256, as said below
- smooth: float32 [27, 27], replicated, may hold values from -1.25 to 1.25
- face_geo: float32 [6, 3, 27], replicated, may hold values from -0.625 to 0.625
- rates: float32 [32, 6, 256], P('dom'), may hold values from 0.1 to 1
- stiff: float32 [27, 27], replicated, may hold values from -1.25 to 1.25
- lift: float32 [6, 27, 27], replicated, may hold values from -1.25 to 1.25
- mass_inv: float32 [27, 27], replicated, may hold values from -1.25 to 1.25
Outputs:
- coords: float32 [32, 3, 2048], P('dom')
- remapped: float32 [32, 5, 27, 256], P('dom')
Inputs may be any that keep to these rules, and one draw needn't show every extreme that they name: Elements from live[p] on are padding; at least one partition is full.
All inputs are finite; a program needn't handle non-finite values.
Results may differ from a plain program's by a relative error of at most 0.0001.
Values sent between devices are 32-bit elements; how exact they have to be, the bound alone decides.
A program may use at most 64 MiB of HBM per device.

v0:
```python
import jax
import jax.numpy as jnp
from jax import lax
from jax.sharding import PartitionSpec as P

SWEEPS = 3
STEPS = 4


relax_factor = 0.5
cfl_number = 0.4
highest = lax.Precision.HIGHEST


def shifted(block, axis, distance):
    devices = range(lax.axis_size(axis))
    route = [((i - distance) % len(devices), i) for i in devices]
    return lax.ppermute(block, axis, route)


def neighbour_offsets(parts):
    stride = max(parts // 8, 1)
    return (1, -1, stride, -stride)


def node_counts(connect, receive, mask, nodes):
    weights = jnp.broadcast_to(mask[None, :], connect.shape).reshape(-1)
    counted = jnp.zeros((nodes,), jnp.float32).at[connect.reshape(-1)].add(weights)
    counted = counted.at[receive.reshape(-1)].add(jnp.ones((receive.size,), jnp.float32))
    return jnp.maximum(counted, 1.0)


def assemble(coords, connect, mask, smooth):
    corner = coords[:, connect]
    smoothed = jnp.einsum("ab,cbe->cae", smooth, corner, precision=highest) * mask[None, None, :]
    flat = smoothed.reshape(coords.shape[0], -1)
    return jnp.zeros(coords.shape, jnp.float32).at[:, connect.reshape(-1)].add(flat)


def face_rates(moved, connect, face_geo, rates, mask):
    corner = moved[:, connect]
    projected = jnp.einsum("fca,cae->fe", face_geo, corner, precision=highest)
    return rates * (1.0 + 0.5 * jnp.tanh(projected)) * mask[None, :]


def face_flux(flux, extended, neighbour, rate, values, lift):
    for face in range(6):
        other = jnp.take(extended, neighbour[face], axis=2)
        flux = flux + rate[face][None, None, :] * jnp.einsum(
            "ab,vbe->vae", lift[face], other - values, precision=highest
        )
    return flux


def finish(values, flux, mask, step_size, mass_inv):
    change = jnp.einsum("ab,vbe->vae", mass_inv, flux, precision=highest)
    return values + step_size * change * mask[None, None, :]


def on_device(
    positions,
    states,
    conn,
    send_nodes,
    recv_nodes,
    send_elems,
    neighbours,
    live,
    smooth,
    face_geo,
    rates,
    stiff,
    lift,
    mass_inv,
):
    shifts = neighbour_offsets(lax.axis_size("dom"))
    start_coords = positions[0]
    values = states[0]
    connect = conn[0]
    sending = send_nodes[0]
    receive = recv_nodes[0]
    ghost_rows = send_elems[0]
    neighbour = neighbours[0]
    elems = connect.shape[-1]
    mask = (jnp.arange(elems) < live[0]).astype(jnp.float32)
    counts = node_counts(connect, receive, mask, start_coords.shape[-1])
    coords = start_coords
    for sweep in range(SWEEPS):
        summed = assemble(coords, connect, mask, smooth)
        total = summed
        for k in range(4):
            arrived = shifted(summed[:, sending[k]], "dom", shifts[k])
            total = total.at[:, receive[k]].add(arrived)
        coords = coords + relax_factor * (total / counts[None, :] - coords)
    rate = face_rates(coords - start_coords, connect, face_geo, rates[0], mask)
    largest = lax.pmax(jnp.max(jnp.sum(rate, axis=0)), "dom")
    step_size = cfl_number / largest
    for step in range(STEPS):
        ghosts = []
        for k in range(4):
            picked = values[:, :, ghost_rows[k]]
            ghosts.append(shifted(picked, "dom", shifts[k]))
        flux = jnp.einsum("ab,vbe->vae", stiff, values, precision=highest)
        extended = jnp.concatenate([values] + ghosts, axis=2)
        flux = face_flux(flux, extended, neighbour, rate, values, lift)
        values = finish(values, flux, mask, step_size, mass_inv)
    return (coords[None], values[None])


def solution(mesh):
    in_specs = (
        P("dom", None, None),
        P("dom", None, None, None),
        P("dom", None, None),
        P("dom", None, None),
        P("dom", None, None),
        P("dom", None, None),
        P("dom", None, None),
        P("dom"),
        P(),
        P(),
        P("dom", None, None),
        P(),
        P(),
        P(),
    )
    out_specs = (P("dom", None, None), P("dom", None, None, None))
    return jax.shard_map(
        on_device, mesh=mesh, in_specs=in_specs, out_specs=out_specs, check_vma=False
    )
```

profile of v0, /device:TPU:0, one launch (start us, length us, event | category | flops | bytes accessed | tf_op | source)
XLA Modules:
  0.0 458.3 jit_solution(14429515281876442598)
XLA Ops:
  3.3 13.5 %gather_fusion = f32[6912,3]{1,0:T(8,128)} fusion(f32[3,2048]{0,1:T(8,128)S(1)} %copy.118, s32[7168]{0:T(1024)S(1)} %pad_clamp_fusion), kind=kCustom, calls=%fused_computation.24 | custom fusion | bytes 193536 | tf_op jit(solution)/shard_map/gather | solution.py:34
  22.4 39.3 %scatter_custom_fusion = f32[3,2048]{0,1:T(8,128)S(1)} fusion(s32[6912]{0:T(1024)S(1)} %fusion.129, f32[6912,3]{1,0:T(8,128)} %bitcast.415, f32[]{:T(128)} %constant.16.clone.1), kind=kCustom, calls=%fused_computation.159 | custom fusion | flops 20736 | bytes 25088 | tf_op jit(solution)/shard_map/scatter-add | solution.py:37
  63.4 6.0 %collective-permute-start.1 = (f32[3,32]{0,1:T(8,128)S(1)}, f32[3,32]{0,1:T(8,128)S(1)}, u32[]{:S(2)}, u32[]{:S(2)}) collective-permute-start(f32[3,32]{0,1:T(8,128)S(1)} %bitcast.478), channel_id=1, source_target_pairs={{1,0},{2,1},{3,2},{4,3},{5,4},{6,5},{7,6},{8,7},{9,8},{10,9},{11,1... | collective-permute-start | bytes 1160 | tf_op jit(solution)/shard_map/ppermute | solution.py:18
  70.6 4.8 %collective-permute-start.3 = (f32[3,32]{0,1:T(8,128)S(1)}, f32[3,32]{0,1:T(8,128)S(1)}, u32[]{:S(2)}, u32[]{:S(2)}) collective-permute-start(f32[3,32]{0,1:T(8,128)S(1)} %bitcast.480), channel_id=1, source_target_pairs={{4,0},{5,1},{6,2},{7,3},{8,4},{9,5},{10,6},{11,7},{12,8},{13,9},{1... | collective-permute-start | bytes 1160 | tf_op jit(solution)/shard_map/ppermute | solution.py:18
  77.9 36.8 %scatter_custom_fusion.5 = f32[2048]{0:T(1024)S(1)} fusion(s32[6912]{0:T(1024)S(1)} %fusion.129, f32[6912]{0:T(1024)S(1)} %reshape.990, f32[]{:T(128)} %constant.16.clone.1), kind=kCustom, calls=%fused_computation.373 | custom fusion | flops 6912 | bytes 8196 | tf_op jit(solution)/shard_map/scatter-add | solution.py:28
  124.1 13.5 %gather_fusion.5 = f32[6912,3]{1,0:T(8,128)} fusion(f32[3,2048]{0,1:T(8,128)S(1)} %copy.122, s32[7168]{0:T(1024)S(1)} %pad_clamp_fusion), kind=kCustom, calls=%fused_computation.29 | custom fusion | bytes 193536 | tf_op jit(solution)/shard_map/gather | solution.py:34
  143.0 39.3 %scatter_custom_fusion.7 = f32[3,2048]{0,1:T(8,128)S(1)} fusion(s32[6912]{0:T(1024)S(1)} %fusion.129, f32[6912,3]{1,0:T(8,128)} %bitcast.417, f32[]{:T(128)} %constant.16.clone.1), kind=kCustom, calls=%fused_computation.157 | custom fusion | flops 20736 | bytes 25088 | tf_op jit(solution)/shard_map/scatter-add | solution.py:37
  184.6 5.4 %collective-permute-start.5 = (f32[3,32]{0,1:T(8,128)S(1)}, f32[3,32]{0,1:T(8,128)S(1)}, u32[]{:S(2)}, u32[]{:S(2)}) collective-permute-start(f32[3,32]{0,1:T(8,128)S(1)} %bitcast.486), channel_id=1, source_target_pairs={{1,0},{2,1},{3,2},{4,3},{5,4},{6,5},{7,6},{8,7},{9,8},{10,9},{11,1... | collective-permute-start | bytes 1160 | tf_op jit(solution)/shard_map/ppermute | solution.py:18
  190.0 4.7 %collective-permute-start.7 = (f32[3,32]{0,1:T(8,128)S(1)}, f32[3,32]{0,1:T(8,128)S(1)}, u32[]{:S(2)}, u32[]{:S(2)}) collective-permute-start(f32[3,32]{0,1:T(8,128)S(1)} %bitcast.483), channel_id=1, source_target_pairs={{4,0},{5,1},{6,2},{7,3},{8,4},{9,5},{10,6},{11,7},{12,8},{13,9},{1... | collective-permute-start | bytes 1160 | tf_op jit(solution)/shard_map/ppermute | solution.py:18
  200.1 13.5 %gather_fusion.10 = f32[6912,3]{1,0:T(8,128)} fusion(f32[3,2048]{0,1:T(8,128)S(1)} %copy.126, s32[7168]{0:T(1024)S(1)} %pad_clamp_fusion), kind=kCustom, calls=%fused_computation.34 | custom fusion | bytes 193536 | tf_op jit(solution)/shard_map/gather | solution.py:34
  219.0 39.3 %scatter_custom_fusion.12 = f32[3,2048]{0,1:T(8,128)S(1)} fusion(s32[6912]{0:T(1024)S(1)} %fusion.129, f32[6912,3]{1,0:T(8,128)} %bitcast.416, f32[]{:T(128)} %constant.16.clone.1), kind=kCustom, calls=%fused_computation.155 | custom fusion | flops 20736 | bytes 25088 | tf_op jit(solution)/shard_map/scatter-add | solution.py:37
  260.6 4.9 %collective-permute-start.9 = (f32[3,32]{0,1:T(8,128)S(1)}, f32[3,32]{0,1:T(8,128)S(1)}, u32[]{:S(2)}, u32[]{:S(2)}) collective-permute-start(f32[3,32]{0,1:T(8,128)S(1)} %bitcast.487), channel_id=1, source_target_pairs={{1,0},{2,1},{3,2},{4,3},{5,4},{6,5},{7,6},{8,7},{9,8},{10,9},{11,1... | collective-permute-start | bytes 1160 | tf_op jit(solution)/shard_map/ppermute | solution.py:18
  266.1 4.7 %collective-permute-start.11 = (f32[3,32]{0,1:T(8,128)S(1)}, f32[3,32]{0,1:T(8,128)S(1)}, u32[]{:S(2)}, u32[]{:S(2)}) collective-permute-start(f32[3,32]{0,1:T(8,128)S(1)} %bitcast.482), channel_id=1, source_target_pairs={{4,0},{5,1},{6,2},{7,3},{8,4},{9,5},{10,6},{11,7},{12,8},{13,9},{1... | collective-permute-start | bytes 1160 | tf_op jit(solution)/shard_map/ppermute | solution.py:18
  273.2 4.7 %collective-permute-start.15 = (f32[5,27,16]{2,1,0:T(8,128)S(1)}, f32[5,27,16]{2,1,0:T(8,128)S(1)}, u32[]{:S(2)}, u32[]{:S(2)}) collective-permute-start(f32[5,27,16]{2,1,0:T(8,128)S(1)} %bitcast.429), channel_id=1, source_target_pairs={{4,0},{5,1},{6,2},{7,3},{8,4},{9,5},{10,6},{11,7},{12,8},{13,9},{1... | collective-permute-start | bytes 25928 | tf_op jit(solution)/shard_map/ppermute | solution.py:18
  281.1 13.5 %gather_fusion.15 = f32[6912,3]{1,0:T(8,128)} fusion(f32[3,2048]{0,1:T(8,128)S(1)} %copy.130, s32[7168]{0:T(1024)S(1)} %pad_clamp_fusion), kind=kCustom, calls=%fused_computation.39 | custom fusion | bytes 193536 | tf_op jit(solution)/shard_map/gather | solution.py:41
  294.6 2.8 copy.131
  298.3 37.0 %pmax.7 = f32[]{:T(128)} all-reduce(f32[]{:T(128)} %reduce_max.9), channel_id=1, replica_groups=mesh['dom'=32] {'dom'}, use_global_device_ids=true, to_apply=%region_19.0 | all-reduce | flops 1 | bytes 8 | tf_op jit(solution)/shard_map/pmax | solution.py:96
  350.7 2.9 collective-permute-start.17
  353.9 4.8 %collective-permute-start.19 = (f32[5,27,16]{2,1,0:T(8,128)S(1)}, f32[5,27,16]{2,1,0:T(8,128)S(1)}, u32[]{:S(2)}, u32[]{:S(2)}) collective-permute-start(f32[5,27,16]{2,1,0:T(8,128)S(1)} %bitcast.438), channel_id=1, source_target_pairs={{4,0},{5,1},{6,2},{7,3},{8,4},{9,5},{10,6},{11,7},{12,8},{13,9},{1... | collective-permute-start | bytes 25928 | tf_op jit(solution)/shard_map/ppermute | solution.py:18
  360.9 5.6 %collective-permute-done.16 = f32[5,27,16]{2,1,0:T(8,128)S(1)} collective-permute-done((f32[5,27,16]{2,1,0:T(8,128)S(1)}, f32[5,27,16]{2,1,0:T(8,128)S(1)}, u32[]{:S(2)}, u32[]{:S(2)}) %collective-permute-start.16) | collective-permute-done | bytes 8672 | tf_op jit(solution)/shard_map/ppermute | solution.py:18
  389.2 4.8 %collective-permute-start.23 = (f32[5,27,16]{2,1,0:T(8,128)S(1)}, f32[5,27,16]{2,1,0:T(8,128)S(1)}, u32[]{:S(2)}, u32[]{:S(2)}) collective-permute-start(f32[5,27,16]{2,1,0:T(8,128)S(1)} %bitcast.439), channel_id=1, source_target_pairs={{4,0},{5,1},{6,2},{7,3},{8,4},{9,5},{10,6},{11,7},{12,8},{13,9},{1... | collective-permute-start | bytes 25928 | tf_op jit(solution)/shard_map/ppermute | solution.py:18
  396.7 5.2 %collective-permute-done.20 = f32[5,27,16]{2,1,0:T(8,128)S(1)} collective-permute-done((f32[5,27,16]{2,1,0:T(8,128)S(1)}, f32[5,27,16]{2,1,0:T(8,128)S(1)}, u32[]{:S(2)}, u32[]{:S(2)}) %collective-permute-start.20) | collective-permute-done | bytes 8672 | tf_op jit(solution)/shard_map/ppermute | solution.py:18
  424.7 4.8 %collective-permute-start.27 = (f32[5,27,16]{2,1,0:T(8,128)S(1)}, f32[5,27,16]{2,1,0:T(8,128)S(1)}, u32[]{:S(2)}, u32[]{:S(2)}) collective-permute-start(f32[5,27,16]{2,1,0:T(8,128)S(1)} %bitcast.434), channel_id=1, source_target_pairs={{4,0},{5,1},{6,2},{7,3},{8,4},{9,5},{10,6},{11,7},{12,8},{13,9},{1... | collective-permute-start | bytes 25928 | tf_op jit(solution)/shard_map/ppermute | solution.py:18
  432.1 5.3 %collective-permute-done.24 = f32[5,27,16]{2,1,0:T(8,128)S(1)} collective-permute-done((f32[5,27,16]{2,1,0:T(8,128)S(1)}, f32[5,27,16]{2,1,0:T(8,128)S(1)}, u32[]{:S(2)}, u32[]{:S(2)}) %collective-permute-start.24) | collective-permute-done | bytes 8672 | tf_op jit(solution)/shard_map/ppermute | solution.py:18
  (322 shorter events, 137.4 us)
Async XLA Ops:
  62.3 55.9 %collective-permute-start = (f32[3,32]{0,1:T(8,128)S(1)}, f32[3,32]{0,1:T(8,128)S(1)}, u32[]{:S(2)}, u32[]{:S(2)}) collective-permute-start(f32[3,32]{0,1:T(8,128)S(1)} %bitcast.479), channel_id=1, source_target_pairs={{31,0},{0,1},{1,2},{2,3},{3,4},{4,5},{5,6},{6,7},{7,8},{8,9},{9,10... | collective-permute-start | bytes 1160 | tf_op jit(solution)/shard_map/ppermute | solution.py:18
  63.4 55.9 %collective-permute-start.1 = (f32[3,32]{0,1:T(8,128)S(1)}, f32[3,32]{0,1:T(8,128)S(1)}, u32[]{:S(2)}, u32[]{:S(2)}) collective-permute-start(f32[3,32]{0,1:T(8,128)S(1)} %bitcast.478), channel_id=1, source_target_pairs={{1,0},{2,1},{3,2},{4,3},{5,4},{6,5},{7,6},{8,7},{9,8},{10,9},{11,1... | collective-permute-start | bytes 1160 | tf_op jit(solution)/shard_map/ppermute | solution.py:18
  69.9 50.5 %collective-permute-start.2 = (f32[3,32]{0,1:T(8,128)S(1)}, f32[3,32]{0,1:T(8,128)S(1)}, u32[]{:S(2)}, u32[]{:S(2)}) collective-permute-start(f32[3,32]{0,1:T(8,128)S(1)} %bitcast.481), channel_id=1, source_target_pairs={{28,0},{29,1},{30,2},{31,3},{0,4},{1,5},{2,6},{3,7},{4,8},{5,9},{6... | collective-permute-start | bytes 1160 | tf_op jit(solution)/shard_map/ppermute | solution.py:18
  70.6 51.1 %collective-permute-start.3 = (f32[3,32]{0,1:T(8,128)S(1)}, f32[3,32]{0,1:T(8,128)S(1)}, u32[]{:S(2)}, u32[]{:S(2)}) collective-permute-start(f32[3,32]{0,1:T(8,128)S(1)} %bitcast.480), channel_id=1, source_target_pairs={{4,0},{5,1},{6,2},{7,3},{8,4},{9,5},{10,6},{11,7},{12,8},{13,9},{1... | collective-permute-start | bytes 1160 | tf_op jit(solution)/shard_map/ppermute | solution.py:18
  76.5 259.4 %collective-permute-start.12 = (f32[5,27,16]{2,1,0:T(8,128)S(1)}, f32[5,27,16]{2,1,0:T(8,128)S(1)}, u32[]{:S(2)}, u32[]{:S(2)}) collective-permute-start(f32[5,27,16]{2,1,0:T(8,128)S(1)} %bitcast.426), channel_id=1, source_target_pairs={{31,0},{0,1},{1,2},{2,3},{3,4},{4,5},{5,6},{6,7},{7,8},{8,9},{9,10... | collective-permute-start | bytes 25928 | tf_op jit(solution)/shard_map/ppermute | solution.py:18
  184.0 10.7 %collective-permute-start.4 = (f32[3,32]{0,1:T(8,128)S(1)}, f32[3,32]{0,1:T(8,128)S(1)}, u32[]{:S(2)}, u32[]{:S(2)}) collective-permute-start(f32[3,32]{0,1:T(8,128)S(1)} %bitcast.488), channel_id=1, source_target_pairs={{31,0},{0,1},{1,2},{2,3},{3,4},{4,5},{5,6},{6,7},{7,8},{8,9},{9,10... | collective-permute-start | bytes 1160 | tf_op jit(solution)/shard_map/ppermute | solution.py:18
  184.6 11.3 %collective-permute-start.5 = (f32[3,32]{0,1:T(8,128)S(1)}, f32[3,32]{0,1:T(8,128)S(1)}, u32[]{:S(2)}, u32[]{:S(2)}) collective-permute-start(f32[3,32]{0,1:T(8,128)S(1)} %bitcast.486), channel_id=1, source_target_pairs={{1,0},{2,1},{3,2},{4,3},{5,4},{6,5},{7,6},{8,7},{9,8},{10,9},{11,1... | collective-permute-start | bytes 1160 | tf_op jit(solution)/shard_map/ppermute | solution.py:18
  190.0 8.2 %collective-permute-start.7 = (f32[3,32]{0,1:T(8,128)S(1)}, f32[3,32]{0,1:T(8,128)S(1)}, u32[]{:S(2)}, u32[]{:S(2)}) collective-permute-start(f32[3,32]{0,1:T(8,128)S(1)} %bitcast.483), channel_id=1, source_target_pairs={{4,0},{5,1},{6,2},{7,3},{8,4},{9,5},{10,6},{11,7},{12,8},{13,9},{1... | collective-permute-start | bytes 1160 | tf_op jit(solution)/shard_map/ppermute | solution.py:18
  194.7 141.1 %collective-permute-start.13 = (f32[5,27,16]{2,1,0:T(8,128)S(1)}, f32[5,27,16]{2,1,0:T(8,128)S(1)}, u32[]{:S(2)}, u32[]{:S(2)}) collective-permute-start(f32[5,27,16]{2,1,0:T(8,128)S(1)} %bitcast.428), channel_id=1, source_target_pairs={{1,0},{2,1},{3,2},{4,3},{5,4},{6,5},{7,6},{8,7},{9,8},{10,9},{11,1... | collective-permute-start | bytes 25928 | tf_op jit(solution)/shard_map/ppermute | solution.py:18
  258.9 7.2 %collective-permute-start.8 = (f32[3,32]{0,1:T(8,128)S(1)}, f32[3,32]{0,1:T(8,128)S(1)}, u32[]{:S(2)}, u32[]{:S(2)}) collective-permute-start(f32[3,32]{0,1:T(8,128)S(1)} %bitcast.489), channel_id=1, source_target_pairs={{31,0},{0,1},{1,2},{2,3},{3,4},{4,5},{5,6},{6,7},{7,8},{8,9},{9,10... | collective-permute-start | bytes 1160 | tf_op jit(solution)/shard_map/ppermute | solution.py:18
  260.6 11.4 %collective-permute-start.9 = (f32[3,32]{0,1:T(8,128)S(1)}, f32[3,32]{0,1:T(8,128)S(1)}, u32[]{:S(2)}, u32[]{:S(2)}) collective-permute-start(f32[3,32]{0,1:T(8,128)S(1)} %bitcast.487), channel_id=1, source_target_pairs={{1,0},{2,1},{3,2},{4,3},{5,4},{6,5},{7,6},{8,7},{9,8},{10,9},{11,1... | collective-permute-start | bytes 1160 | tf_op jit(solution)/shard_map/ppermute | solution.py:18
  266.0 7.1 %collective-permute-start.10 = (f32[3,32]{0,1:T(8,128)S(1)}, f32[3,32]{0,1:T(8,128)S(1)}, u32[]{:S(2)}, u32[]{:S(2)}) collective-permute-start(f32[3,32]{0,1:T(8,128)S(1)} %bitcast.485), channel_id=1, source_target_pairs={{28,0},{29,1},{30,2},{31,3},{0,4},{1,5},{2,6},{3,7},{4,8},{5,9},{6... | collective-permute-start | bytes 1160 | tf_op jit(solution)/shard_map/ppermute | solution.py:18
  266.1 13.0 %collective-permute-start.11 = (f32[3,32]{0,1:T(8,128)S(1)}, f32[3,32]{0,1:T(8,128)S(1)}, u32[]{:S(2)}, u32[]{:S(2)}) collective-permute-start(f32[3,32]{0,1:T(8,128)S(1)} %bitcast.482), channel_id=1, source_target_pairs={{4,0},{5,1},{6,2},{7,3},{8,4},{9,5},{10,6},{11,7},{12,8},{13,9},{1... | collective-permute-start | bytes 1160 | tf_op jit(solution)/shard_map/ppermute | solution.py:18
  272.0 63.9 %collective-permute-start.14 = (f32[5,27,16]{2,1,0:T(8,128)S(1)}, f32[5,27,16]{2,1,0:T(8,128)S(1)}, u32[]{:S(2)}, u32[]{:S(2)}) collective-permute-start(f32[5,27,16]{2,1,0:T(8,128)S(1)} %bitcast.427), channel_id=1, source_target_pairs={{28,0},{29,1},{30,2},{31,3},{0,4},{1,5},{2,6},{3,7},{4,8},{5,9},{6... | collective-permute-start | bytes 25928 | tf_op jit(solution)/shard_map/ppermute | solution.py:18
  273.2 62.7 %collective-permute-start.15 = (f32[5,27,16]{2,1,0:T(8,128)S(1)}, f32[5,27,16]{2,1,0:T(8,128)S(1)}, u32[]{:S(2)}, u32[]{:S(2)}) collective-permute-start(f32[5,27,16]{2,1,0:T(8,128)S(1)} %bitcast.429), channel_id=1, source_target_pairs={{4,0},{5,1},{6,2},{7,3},{8,4},{9,5},{10,6},{11,7},{12,8},{13,9},{1... | collective-permute-start | bytes 25928 | tf_op jit(solution)/shard_map/ppermute | solution.py:18
  350.7 8.3 %collective-permute-start.17 = (f32[5,27,16]{2,1,0:T(8,128)S(1)}, f32[5,27,16]{2,1,0:T(8,128)S(1)}, u32[]{:S(2)}, u32[]{:S(2)}) collective-permute-start(f32[5,27,16]{2,1,0:T(8,128)S(1)} %bitcast.432), channel_id=1, source_target_pairs={{1,0},{2,1},{3,2},{4,3},{5,4},{6,5},{7,6},{8,7},{9,8},{10,9},{11,1... | collective-permute-start | bytes 25928 | tf_op jit(solution)/shard_map/ppermute | solution.py:18
  353.7 7.2 %collective-permute-start.18 = (f32[5,27,16]{2,1,0:T(8,128)S(1)}, f32[5,27,16]{2,1,0:T(8,128)S(1)}, u32[]{:S(2)}, u32[]{:S(2)}) collective-permute-start(f32[5,27,16]{2,1,0:T(8,128)S(1)} %bitcast.435), channel_id=1, source_target_pairs={{28,0},{29,1},{30,2},{31,3},{0,4},{1,5},{2,6},{3,7},{4,8},{5,9},{6... | collective-permute-start | bytes 25928 | tf_op jit(solution)/shard_map/ppermute | solution.py:18
  358.7 7.7 %collective-permute-start.16 = (f32[5,27,16]{2,1,0:T(8,128)S(1)}, f32[5,27,16]{2,1,0:T(8,128)S(1)}, u32[]{:S(2)}, u32[]{:S(2)}) collective-permute-start(f32[5,27,16]{2,1,0:T(8,128)S(1)} %bitcast.440), channel_id=1, source_target_pairs={{31,0},{0,1},{1,2},{2,3},{3,4},{4,5},{5,6},{6,7},{7,8},{8,9},{9,10... | collective-permute-start | bytes 25928 | tf_op jit(solution)/shard_map/ppermute | solution.py:18
  389.1 7.6 %collective-permute-start.22 = (f32[5,27,16]{2,1,0:T(8,128)S(1)}, f32[5,27,16]{2,1,0:T(8,128)S(1)}, u32[]{:S(2)}, u32[]{:S(2)}) collective-permute-start(f32[5,27,16]{2,1,0:T(8,128)S(1)} %bitcast.436), channel_id=1, source_target_pairs={{28,0},{29,1},{30,2},{31,3},{0,4},{1,5},{2,6},{3,7},{4,8},{5,9},{6... | collective-permute-start | bytes 25928 | tf_op jit(solution)/shard_map/ppermute | solution.py:18
  389.2 7.4 %collective-permute-start.23 = (f32[5,27,16]{2,1,0:T(8,128)S(1)}, f32[5,27,16]{2,1,0:T(8,128)S(1)}, u32[]{:S(2)}, u32[]{:S(2)}) collective-permute-start(f32[5,27,16]{2,1,0:T(8,128)S(1)} %bitcast.439), channel_id=1, source_target_pairs={{4,0},{5,1},{6,2},{7,3},{8,4},{9,5},{10,6},{11,7},{12,8},{13,9},{1... | collective-permute-start | bytes 25928 | tf_op jit(solution)/shard_map/ppermute | solution.py:18
  394.1 7.8 %collective-permute-start.20 = (f32[5,27,16]{2,1,0:T(8,128)S(1)}, f32[5,27,16]{2,1,0:T(8,128)S(1)}, u32[]{:S(2)}, u32[]{:S(2)}) collective-permute-start(f32[5,27,16]{2,1,0:T(8,128)S(1)} %bitcast.441), channel_id=1, source_target_pairs={{31,0},{0,1},{1,2},{2,3},{3,4},{4,5},{5,6},{6,7},{7,8},{8,9},{9,10... | collective-permute-start | bytes 25928 | tf_op jit(solution)/shard_map/ppermute | solution.py:18
  424.5 7.6 %collective-permute-start.26 = (f32[5,27,16]{2,1,0:T(8,128)S(1)}, f32[5,27,16]{2,1,0:T(8,128)S(1)}, u32[]{:S(2)}, u32[]{:S(2)}) collective-permute-start(f32[5,27,16]{2,1,0:T(8,128)S(1)} %bitcast.431), channel_id=1, source_target_pairs={{28,0},{29,1},{30,2},{31,3},{0,4},{1,5},{2,6},{3,7},{4,8},{5,9},{6... | collective-permute-start | bytes 25928 | tf_op jit(solution)/shard_map/ppermute | solution.py:18
  424.7 7.4 %collective-permute-start.27 = (f32[5,27,16]{2,1,0:T(8,128)S(1)}, f32[5,27,16]{2,1,0:T(8,128)S(1)}, u32[]{:S(2)}, u32[]{:S(2)}) collective-permute-start(f32[5,27,16]{2,1,0:T(8,128)S(1)} %bitcast.434), channel_id=1, source_target_pairs={{4,0},{5,1},{6,2},{7,3},{8,4},{9,5},{10,6},{11,7},{12,8},{13,9},{1... | collective-permute-start | bytes 25928 | tf_op jit(solution)/shard_map/ppermute | solution.py:18
  429.6 7.8 %collective-permute-start.24 = (f32[5,27,16]{2,1,0:T(8,128)S(1)}, f32[5,27,16]{2,1,0:T(8,128)S(1)}, u32[]{:S(2)}, u32[]{:S(2)}) collective-permute-start(f32[5,27,16]{2,1,0:T(8,128)S(1)} %bitcast.437), channel_id=1, source_target_pairs={{31,0},{0,1},{1,2},{2,3},{3,4},{4,5},{5,6},{6,7},{7,8},{8,9},{9,10... | collective-permute-start | bytes 25928 | tf_op jit(solution)/shard_map/ppermute | solution.py:18
  (38 other events, 1471.4 us)
where the time goes:
time: 465 us; the launch traced here: 458 us
  other arithmetic  173 us (37%)
  local copies, waits for them, and re-layouts  157 us (34%)
  starting transfers between devices  54.9 us (12%)
  blocking collectives  37 us (8%)
  waiting for transfers between devices  21.7 us (5%)
  matrix products  10.7 us (2%)
    scatter-add x3, other arithmetic, assemble(): jnp.zeros(coords.shape, jnp.float32).at[:, connect.reshape(-1)].add(flat)  118 us
    gather x48, local copies, waits for them, and re-layouts, face_flux(): other = jnp.take(extended, neighbour[face], axis=2)  57.6 us
    ppermute x28, starting transfers between devices, shifted(): return lax.ppermute(block, axis, route)  54.9 us
    gather x6, local copies, waits for them, and re-layouts, assemble(): corner = coords[:, connect]  48.7 us
    pmax x1, blocking collectives, on_device(): largest = lax.pmax(jnp.max(jnp.sum(rate, axis=0)), 'dom')  37 us
    scatter-add x1, other arithmetic, node_counts(): jnp.zeros((nodes,), jnp.float32).at[connect.reshape(-1)].add(weights)  36.8 us
    ppermute x28, waiting for transfers between devices, shifted(): return lax.ppermute(block, axis, route)  21.7 us
    gather x2, local copies, waits for them, and re-layouts, face_rates(): corner = moved[:, connect]  16.3 us
  transfers between devices with their start and end apart: 28, of which 6 were waited for; matrix products, arithmetic and copies ran while one was open for 44% of the time, Pallas kernels for 0%

commit v1 on v0

v1 whole, which is shorter than its diff:
```python
import functools

import jax
import jax.numpy as jnp
from jax import lax
from jax.experimental import pallas as pl
from jax.experimental.pallas import tpu as pltpu
from jax.sharding import PartitionSpec as P

SWEEPS = 3
STEPS = 4
CFL = 0.4
F32 = jnp.float32
BF16 = jnp.bfloat16
HIGHEST = lax.Precision.HIGHEST
MESH = pl.DeviceIdType.MESH
LANES = 128
ROWS = 32
RADIX = 32


def rounds_of(parts):
    found, stride = [], 1
    while parts > 1:
        radix = max(r for r in range(1, RADIX + 1) if parts % r == 0)
        if radix == 1:
            radix = parts
        found.append((radix, stride))
        stride *= radix
        parts //= radix
    return found


def pick(table, index):
    return jnp.take_along_axis(table, index, axis=1, mode="promise_in_bounds")


def split(x):
    high = x.astype(BF16)
    low = (x - high.astype(F32)).astype(BF16)
    return high, low


def mm(a, b):
    return jnp.dot(a, b, preferred_element_type=F32)


def mm3(a, b):
    high, low = split(b)
    return mm(a[0], high) + (mm(a[1], high) + mm(a[0], low))


def mm_nt(a, b):
    return lax.dot_general(a, b, (((1,), (1,)), ((), ())), preferred_element_type=F32)


def iota(shape, dim):
    return lax.broadcasted_iota(jnp.int32, shape, dim)


def kernel(
    parts, shifts, rounds,
    pos, states, conn, send_nodes, recv_nodes, send_elems, neighbours, live,
    smooth, face_geo, rates, stiff, lift, mass_inv,
    out_c, out_u,
    x_ref, x0_ref, s_ref, lo_ref, hi_ref, y_ref, z_ref, b_ref, rb_ref,
    u_ref, nb_ref, rate_ref, pad_ref, fg_ref, w_ref, idx_ref,
    v_send, v_recv, g_send, g_recv, m_send, m_recv,
    vs_sem, vr_sem, gs_sem, gr_sem, ms_sem, mr_sem,
):
    me = lax.axis_index("dom")
    basis, elems = conn.shape[1], conn.shape[2]
    fields = states.shape[1]
    faces = neighbours.shape[1]
    nodes = pos.shape[2]
    groups = nodes // LANES
    halves = elems // LANES
    shared = send_nodes.shape[2]
    ghosts = send_elems.shape[2]
    slots = LANES // ghosts

    partners = []
    for radix, stride in rounds:
        digit = lax.rem(me // stride, radix)
        partners.append(
            [me + (lax.rem(digit + j, radix) - digit) * stride for j in range(1, radix)]
        )
    targets = [lax.rem(me + o + parts, parts) for o in shifts]

    barrier = pltpu.get_barrier_semaphore()
    greeted = targets + [t for one in partners for t in one]
    for t in greeted:
        pl.semaphore_signal(barrier, inc=1, device_id=(t,), device_id_type=MESH)

    u_ref[...] = jnp.zeros(u_ref.shape, F32)
    for v in range(fields):
        u_ref[v * ROWS : v * ROWS + basis, :] = states[0, v]

    lane = iota((8, LANES), 1)
    row = iota((8, LANES), 0)
    idx_ref[...] = jnp.zeros(idx_ref.shape, jnp.int32)
    idx_ref[0:4, 0:shared] = send_nodes[0]
    idx_ref[8:12, 0:shared] = recv_nodes[0]
    idx_ref[16:20, 0:ghosts] = send_elems[0]

    def flat(block):
        spread = pick(block, lax.rem(lane, shared))
        kept = jnp.where(lane // shared == row, spread, 0)
        return jnp.sum(kept, axis=0, keepdims=True)

    sent_nodes = flat(idx_ref[0:8, :])
    got_nodes = flat(idx_ref[8:16, :])
    idx_ref[16:24, :] = pick(idx_ref[16:24, :], lax.rem(lane, ghosts))

    slot_of = iota((ROWS, LANES), 1) // ghosts

    def pack_ghosts(step):
        for k in range(4):
            which = jnp.broadcast_to(idx_ref[16 + k : 17 + k, :], (ROWS, LANES))
            low = which & (LANES - 1)
            far = which >> 7
            tile = jnp.zeros((ROWS, LANES), F32)
            for v in range(fields):
                got = pick(u_ref[v * ROWS : (v + 1) * ROWS, 0:LANES], low)
                for h in range(1, halves):
                    other = pick(u_ref[v * ROWS : (v + 1) * ROWS, h * LANES : (h + 1) * LANES], low)
                    got = jnp.where(far == h, other, got)
                tile = jnp.where(slot_of == (v + k) % slots, got, tile)
            g_send[step, k] = tile

    def ghost_copy(step, k):
        return pltpu.make_async_remote_copy(
            src_ref=g_send.at[step, k], dst_ref=g_recv.at[step, k],
            send_sem=gs_sem.at[step, k], recv_sem=gr_sem.at[step, k],
            device_id=(targets[k],), device_id_type=MESH,
        )

    def node_copy(sweep, k):
        return pltpu.make_async_remote_copy(
            src_ref=v_send.at[sweep], dst_ref=v_recv.at[sweep, k],
            send_sem=vs_sem.at[sweep, k], recv_sem=vr_sem.at[sweep, k],
            device_id=(targets[k],), device_id_type=MESH,
        )

    def most_copy(r, j):
        at = sum(len(p) for p in partners[:r]) + j
        return pltpu.make_async_remote_copy(
            src_ref=m_send.at[r], dst_ref=m_recv.at[at],
            send_sem=ms_sem.at[at], recv_sem=mr_sem.at[at],
            device_id=(partners[r][j],), device_id_type=MESH,
        )

    pack_ghosts(0)

    for c in range(3):
        for g in range(groups):
            r = c * groups + g
            x0_ref[r : r + 1, :] = pos[0, c : c + 1, g * LANES : (g + 1) * LANES]
    x_ref[...] = x0_ref[...]
    s_ref[...] = jnp.zeros(s_ref.shape, F32)

    alive = (iota((1, elems), 1) < live[0])
    lo_ref[...] = jnp.zeros(lo_ref.shape, jnp.int32)
    hi_ref[...] = jnp.zeros(hi_ref.shape, jnp.int32)
    lo_ref[0:basis, :] = conn[0] & (LANES - 1)
    hi_ref[0:basis, :] = conn[0] >> 7

    sub_lo = iota((LANES, elems), 0)
    sub_hi = iota((groups, elems), 0)
    one_lo, one_hi = jnp.float32(1.0), jnp.float32(1.0)
    for a in range(basis):
        at = pl.ds(a * elems, elems)
        b_ref[:, at] = jnp.where(sub_lo == lo_ref[a : a + 1, :], one_lo, 0.0).astype(BF16)
        z_ref[0:groups, at] = jnp.where(
            jnp.where(alive, hi_ref[a : a + 1, :], groups) == sub_hi, one_hi, 0.0
        ).astype(BF16)
    got_lo, got_hi = got_nodes & (LANES - 1), got_nodes >> 7
    rb_ref[...] = jnp.where(iota((LANES, LANES), 0) == got_lo, one_lo, 0.0).astype(BF16)
    got_mask = iota((groups, LANES), 0) == got_hi
    count = mm_nt(z_ref[0:groups, :], b_ref[...])
    count = count + mm_nt(jnp.where(got_mask, one_hi, 0.0).astype(BF16), rb_ref[...])
    half_inv = 0.5 / jnp.maximum(count, 1.0)
    half_inv = jnp.concatenate([half_inv] * 3, axis=0)

    pl.semaphore_wait(barrier, len(greeted))
    for k in range(4):
        ghost_copy(0, k).start()

    pad_ref[...] = jnp.zeros(pad_ref.shape, F32)
    for i in range(faces + 1):
        matrix = stiff[...] if i == 0 else lift[i - 1]
        pad_ref[i * ROWS : i * ROWS + basis, 0:basis] = jnp.dot(
            mass_inv[...], matrix, precision=HIGHEST, preferred_element_type=F32
        )
    wide = []
    for first in range(0, faces + 1, 4):
        total = None
        for i in range(first, min(first + 4, faces + 1)):
            block = pad_ref[i * ROWS : (i + 1) * ROWS, :]
            if i > first:
                block = pltpu.roll(block, ROWS * (i - first), 1)
            total = block if total is None else total + block
        wide.append(total)
    w_high, w_low = split(jnp.concatenate(wide, axis=1))
    w_ref[0:ROWS, :] = w_high
    w_ref[ROWS : 2 * ROWS, :] = w_low
    pad_ref[0:ROWS, :] = jnp.zeros((ROWS, LANES), F32)
    pad_ref[0:basis, 0:basis] = smooth[...]
    smooth_parts = split(pad_ref[0:ROWS, 0:ROWS])
    fg_ref[...] = jnp.zeros(fg_ref.shape, F32)
    for c in range(3):
        fg_ref[c * 8 : c * 8 + faces, 0:basis] = face_geo[:, c, :]

    def corners(table):
        result = []
        for c in range(3):
            cols = []
            for h in range(halves):
                low = lo_ref[:, h * LANES : (h + 1) * LANES]
                high = hi_ref[:, h * LANES : (h + 1) * LANES]
                value = jnp.zeros((ROWS, LANES), F32)
                for g in range(groups):
                    r = c * groups + g
                    source = jnp.broadcast_to(table[r : r + 1, :], (ROWS, LANES))
                    value = jnp.where(high == g, pick(source, low), value)
                cols.append(value)
            result.append(jnp.concatenate(cols, axis=1))
        return result

    s_low = jnp.broadcast_to(sent_nodes & (LANES - 1), (8, LANES))
    s_high = jnp.broadcast_to(sent_nodes >> 7, (8, LANES))

    for sweep in range(SWEEPS):
        near = corners(x_ref)
        for c in range(3):
            y = mm3(smooth_parts, near[c])
            y_high = y.astype(BF16).astype(F32)
            y_ref[c * ROWS : (c + 1) * ROWS, :] = y_high
            y_ref[(3 + c) * ROWS : (4 + c) * ROWS, :] = y - y_high
        for a in range(basis):
            at = pl.ds(a * elems, elems)
            chosen = jnp.where(alive, hi_ref[a : a + 1, :], groups) == sub_hi
            for i in range(6):
                z_ref[i * groups : (i + 1) * groups, at] = jnp.where(
                    chosen, y_ref[i * ROWS + a : i * ROWS + a + 1, :], 0.0
                ).astype(BF16)
        both = mm_nt(z_ref[...], b_ref[...])
        sums = both[0 : 3 * groups] + both[3 * groups :]
        for c in range(3):
            for g in range(groups):
                r = c * groups + g
                s_ref[g * 8 + c : g * 8 + c + 1, :] = sums[r : r + 1, :]
        picked = jnp.zeros((8, LANES), F32)
        for g in range(groups):
            picked = jnp.where(s_high == g, pick(s_ref[g * 8 : g * 8 + 8, :], s_low), picked)
        v_send[sweep] = jnp.where(row < 3, picked, 0.0)
        for k in range(4):
            node_copy(sweep, k).start()
        for k in range(4):
            node_copy(sweep, k).wait_recv()
        arrived = v_recv[sweep, 0]
        for k in range(1, 4):
            arrived = jnp.where(lane // shared == k, v_recv[sweep, k], arrived)
        arr_high = arrived.astype(BF16).astype(F32)
        arr_low = arrived - arr_high
        pieces = [
            jnp.where(got_mask, part[c : c + 1, :], 0.0).astype(BF16)
            for part in (arr_high, arr_low) for c in range(3)
        ]
        both = mm_nt(jnp.concatenate(pieces, axis=0), rb_ref[...])
        sums = sums + (both[0 : 3 * groups] + both[3 * groups :])
        x_ref[...] = 0.5 * x_ref[...] + sums * half_inv

    for c in range(3):
        for g in range(groups):
            r = c * groups + g
            out_c[0, c : c + 1, g * LANES : (g + 1) * LANES] = x_ref[r : r + 1, :]

    x_ref[...] = x_ref[...] - x0_ref[...]
    near = corners(x_ref)
    projected = jnp.zeros((8, elems), F32)
    for c in range(3):
        projected = projected + mm3(split(fg_ref[c * 8 : c * 8 + 8, 0:ROWS]), near[c])
    rate = rates[0] * (1.0 + 0.5 * jnp.tanh(projected[0:faces])) * jnp.where(alive, 1.0, 0.0)
    rate_ref[0:faces, :] = rate
    most = jnp.max(jnp.sum(rate, axis=0, keepdims=True), axis=1, keepdims=True)
    m_send[0] = jnp.broadcast_to(most, (8, LANES))
    for j in range(len(partners[0]) if rounds else 0):
        most_copy(0, j).start()

    def gather_local():
        for v in range(fields):
            for h in range(halves):
                for f in range(faces):
                    which = jnp.broadcast_to(
                        neighbours[0, f : f + 1, h * LANES : (h + 1) * LANES], (ROWS, LANES)
                    )
                    low, far = which & (LANES - 1), which >> 7
                    got = pick(u_ref[v * ROWS : (v + 1) * ROWS, 0:LANES], low)
                    for s in range(1, halves):
                        other = pick(u_ref[v * ROWS : (v + 1) * ROWS, s * LANES : (s + 1) * LANES], low)
                        got = jnp.where(far == s, other, got)
                    r = (v * faces + f) * ROWS
                    nb_ref[r : r + ROWS, h * LANES : (h + 1) * LANES] = got

    def change_of(step, v):
        ghost = g_recv[step, 0]
        for k in range(1, 4):
            ghost = jnp.where(slot_of == (v + k) % slots, g_recv[step, k], ghost)
        u = u_ref[v * ROWS : (v + 1) * ROWS, :]
        stack = [u]
        for f in range(faces):
            cols = []
            r = (v * faces + f) * ROWS
            for h in range(halves):
                which = jnp.broadcast_to(
                    neighbours[0, f : f + 1, h * LANES : (h + 1) * LANES], (ROWS, LANES)
                )
                got = pick(ghost, (which + ghosts * v) & (LANES - 1))
                cols.append(jnp.where(which >= elems, got, nb_ref[r : r + ROWS, h * LANES : (h + 1) * LANES]))
            stack.append(rate_ref[f : f + 1, :] * (jnp.concatenate(cols, axis=1) - u))
        high, low = split(jnp.concatenate(stack, axis=0))
        depth = (faces + 1) * ROWS
        first = mm(w_ref[:, 0:depth], high)
        return first[0:ROWS] + (first[ROWS:] + mm(w_ref[0:ROWS, 0:depth], low))

    for step in range(STEPS):
        if step > 0:
            pack_ghosts(step)
            for k in range(4):
                ghost_copy(step, k).start()
        gather_local()
        for k in range(4):
            ghost_copy(step, k).wait_recv()
        changes = [change_of(step, v) for v in range(fields)]
        if step == 0:
            for r, one in enumerate(partners):
                if r > 0:
                    m_send[r] = jnp.broadcast_to(most, (8, LANES))
                    for j in range(len(one)):
                        most_copy(r, j).start()
                at = sum(len(p) for p in partners[:r])
                for j in range(len(one)):
                    most_copy(r, j).wait_recv()
                tile = m_send[r]
                for j in range(len(one)):
                    tile = jnp.maximum(tile, m_recv[at + j])
                most = tile[0:1, 0:1]
            scale = jnp.where(alive, CFL / most, 0.0)
        for v in range(fields):
            new = u_ref[v * ROWS : (v + 1) * ROWS, :] + scale * changes[v]
            if step < STEPS - 1:
                u_ref[v * ROWS : (v + 1) * ROWS, :] = new
            else:
                out_u[0, v] = new[0:basis, :]

    for sweep in range(SWEEPS):
        for k in range(4):
            node_copy(sweep, k).wait_send()
    for step in range(STEPS):
        for k in range(4):
            ghost_copy(step, k).wait_send()
    for r, one in enumerate(partners):
        for j in range(len(one)):
            most_copy(r, j).wait_send()


def on_device(*args):
    pos, states, conn = args[:3]
    parts = lax.axis_size("dom")
    w = max(parts // 8, 1)
    shifts = (1, -1, w, -w)
    rounds = rounds_of(parts)
    total = sum(r - 1 for r, _ in rounds)
    basis, elems = conn.shape[1:]
    fields, faces = states.shape[1], args[6].shape[1]
    groups = pos.shape[2] // LANES
    vmem = pl.BlockSpec(memory_space=pltpu.VMEM)
    smem = pl.BlockSpec(memory_space=pltpu.SMEM)
    specs = [smem if i == 7 else vmem for i in range(len(args))]
    scratch = [
        pltpu.VMEM((3 * groups, LANES), F32),
        pltpu.VMEM((3 * groups, LANES), F32),
        pltpu.VMEM((8 * groups, LANES), F32),
        pltpu.VMEM((ROWS, elems), jnp.int32),
        pltpu.VMEM((ROWS, elems), jnp.int32),
        pltpu.VMEM((6 * ROWS, elems), F32),
        pltpu.VMEM((6 * groups, basis * elems), BF16),
        pltpu.VMEM((LANES, basis * elems), BF16),
        pltpu.VMEM((LANES, LANES), BF16),
        pltpu.VMEM((fields * ROWS, elems), F32),
        pltpu.VMEM((fields * faces * ROWS, elems), F32),
        pltpu.VMEM((8, elems), F32),
        pltpu.VMEM(((faces + 1) * ROWS, LANES), F32),
        pltpu.VMEM((24, LANES), F32),
        pltpu.VMEM((2 * ROWS, 2 * LANES), BF16),
        pltpu.VMEM((24, LANES), jnp.int32),
        pltpu.VMEM((SWEEPS, 8, LANES), F32),
        pltpu.VMEM((SWEEPS, 4, 8, LANES), F32),
        pltpu.VMEM((STEPS, 4, ROWS, LANES), F32),
        pltpu.VMEM((STEPS, 4, ROWS, LANES), F32),
        pltpu.VMEM((max(len(rounds), 1), 8, LANES), F32),
        pltpu.VMEM((max(total, 1), 8, LANES), F32),
        pltpu.SemaphoreType.DMA((SWEEPS, 4)),
        pltpu.SemaphoreType.DMA((SWEEPS, 4)),
        pltpu.SemaphoreType.DMA((STEPS, 4)),
        pltpu.SemaphoreType.DMA((STEPS, 4)),
        pltpu.SemaphoreType.DMA((max(total, 1),)),
        pltpu.SemaphoreType.DMA((max(total, 1),)),
    ]
    return pl.pallas_call(
        functools.partial(kernel, parts, shifts, rounds),
        out_shape=(
            jax.ShapeDtypeStruct(pos.shape, F32),
            jax.ShapeDtypeStruct(states.shape, F32),
        ),
        in_specs=specs,
        out_specs=(vmem, vmem),
        scratch_shapes=scratch,
        compiler_params=pltpu.CompilerParams(
            collective_id=0, has_side_effects=True, vmem_limit_bytes=32 * 1024 * 1024
        ),
    )(*args)


def solution(mesh):
    dom = lambda rank: P("dom", *([None] * (rank - 1)))
    in_specs = (
        dom(3), dom(4), dom(3), dom(3), dom(3), dom(3), dom(3), P("dom"),
        P(), P(), dom(3), P(), P(), P(),
    )
    return jax.shard_map(
        on_device, mesh=mesh, in_specs=in_specs, out_specs=(dom(3), dom(4)), check_vma=False
    )
```

time: 465 us -> 55.5 us (0.12); the launches traced: 458 us -> 55.1 us
  other arithmetic: 173 us -> 0 us
  local copies, waits for them, and re-layouts: 157 us -> 5.17 us
  starting transfers between devices: 54.9 us -> 0 us
  Pallas kernels: 0 us -> 48.5 us
  blocking collectives: 37 us -> 0 us
  waiting for transfers between devices: 21.7 us -> 0 us
  matrix products: 10.7 us -> 0 us
    scatter-add x17 -> x0, other arithmetic: 170 us -> none  [the longest x3 118 us: assemble(): jnp.zeros(coords.shape, jnp.float32).at[:, connect.reshape(-1)].add(flat)]
    gather x100 -> x0, local copies, waits for them, and re-layouts: 140 us -> none  [the longest x48 57.6 us: face_flux(): other = jnp.take(extended, neighbour[face], axis=2)]
    ppermute x28 -> x0, starting transfers between devices: 54.9 us -> none  [shifted(): return lax.ppermute(block, axis, route)]
    pallas_call x0 -> x1, Pallas kernels: none -> 48.5 us  [on_device(): pl.pallas_call(functools.partial(kernel, parts, shifts, rounds), out_shap...]
    pmax x1 -> x0, blocking collectives: 37 us -> none  [on_device(): largest = lax.pmax(jnp.max(jnp.sum(rate, axis=0)), 'dom')]
    ppermute x28 -> x0, waiting for transfers between devices: 21.7 us -> none  [shifted(): return lax.ppermute(block, axis, route)]
    dot_general x36 -> x0, matrix products: 10.7 us -> none  [the longest x24 7.33 us: face_flux(): jnp.einsum('ab,vbe->vae', lift[face], other - values, precision=highest)]
    reshape x4 -> x0, local copies, waits for them, and re-layouts: 7.29 us -> none  [the longest x3 7.29 us: assemble(): flat = smoothed.reshape(coords.shape[0], -1)]
  transfers between devices with their start and end apart: 28 -> 0, of which waited for: 6 -> 0; matrix products, arithmetic and copies ran while one was open for 44% -> 0% of each run, Pallas kernels for 0% -> 0%
where the time goes in v1:
time: 55.5 us; the launch traced here: 55.1 us
  Pallas kernels  48.5 us (87%)
  local copies, waits for them, and re-layouts  5.17 us (9%)
  between operations  1.42 us (3%)
    pallas_call x1, Pallas kernels, on_device(): pl.pallas_call(functools.partial(kernel, parts, shifts, rounds), out_shap...  48.5 us
    unnamed x23, local copies, waits for them, and re-layouts  3.74 us
    pallas_call x2, local copies, waits for them, and re-layouts, on_device(): pl.pallas_call(functools.partial(kernel, parts, shifts, rounds), out_shap...  1.43 us

profile of v1, /device:TPU:0, one launch (start us, length us, event | category | flops | bytes accessed | tf_op | source)
XLA Modules:
  0.0 55.1 jit_solution(10444392216541075036)
XLA Ops:
  0.6 0.0 copy-start.8
  1.3 0.7 %copy.19.neighbours = s32[1,6,256]{2,1,0:T(8,128)S(1)} copy(s32[1,6,256]{2,0,1:T(1,128)} %param.20) | data formatting | bytes 12288 | tf_op args[6]
  2.0 0.7 %copy.20.rates = f32[1,6,256]{2,1,0:T(8,128)S(1)} copy(f32[1,6,256]{2,0,1:T(1,128)} %param.24) | data formatting | bytes 12288 | tf_op args[10]
  2.7 0.8 %copy.16.pos = f32[1,3,2048]{2,1,0:T(4,128)S(1)} copy(f32[1,3,2048]{2,0,1:T(1,128)} %param.14) | data formatting | bytes 49152 | tf_op args[0]
  3.5 0.8 %copy.18.conn = s32[1,27,256]{2,1,0:T(8,128)S(1)} copy(s32[1,27,256]{2,0,1:T(1,128)} %param.16) | data formatting | bytes 55296 | tf_op args[2]
  4.2 0.0 copy-done.8
  4.2 0.0 copy-start
  4.2 0.0 copy-start.2
  4.2 0.0 copy-start.3
  4.3 0.0 copy-start.4
  4.3 0.0 copy-start.5
  4.3 0.0 copy-start.6
  4.3 0.0 copy-start.7
  4.3 0.8 %copy-done = f32[6,27,27]{2,1,0:T(8,128)S(1)} copy-done((f32[6,27,27]{2,1,0:T(8,128)S(1)}, f32[6,27,27]{2,1,0:T(8,128)}, u32[]{:S(2)}) %copy-start) | copy-done | bytes 17520
  5.1 0.0 copy-done.1
  5.1 0.0 copy-done.2
  5.1 0.0 copy-done.3
  5.1 0.0 copy-done.4
  5.1 0.0 copy-done.5
  5.1 0.0 copy-done.6
  5.1 0.0 copy-done.7
  5.2 48.5 %shard_map.149 = (f32[1,3,2048]{2,1,0:T(4,128)S(1)}, f32[1,5,27,256]{3,2,1,0:T(8,128)S(1)}) custom-call(f32[1,3,2048]{2,1,0:T(4,128)S(1)} %copy.16.pos, f32[1,5,27,256]{3,2,1,0:T(8,128)S(1)} %copy.17.states, s32[1,27,256]{2,1,0:T(8,128)S(1)} %copy.18.conn, s32[1,4,32]{2,1,0:T(4,128)S(1)} %copy-done.5, s32[1,4,32]{2,1,0:T(4,128)S(1)} %copy-done.6, ...), custom_call_target="tpu_custom_call" | custom-call | tf_op jit(solution)/shard_map/pallas_call | solution.py:411
  53.7 0.6 %copy.21 = f32[1,3,2048]{2,0,1:T(1,128)} copy(f32[1,3,2048]{2,1,0:T(4,128)S(1)} %get-tuple-element.2) | data formatting | bytes 49152 | tf_op jit(solution)/shard_map/pallas_call | solution.py:411
  54.3 0.8 %copy.22 = f32[1,5,27,256]{3,0,2,1:T(1,128)} copy(f32[1,5,27,256]{3,2,1,0:T(8,128)S(1)} %get-tuple-element.3) | data formatting | bytes 276480 | tf_op jit(solution)/shard_map/pallas_call | solution.py:411
  (2 shorter events, 0.0 us)
Async XLA Ops:
  0.6 3.6 %copy-start.8 = (f32[1,5,27,256]{3,0,2,1:T(1,128)S(1)}, f32[1,5,27,256]{3,0,2,1:T(1,128)}, u32[]{:S(2)}) copy-start(f32[1,5,27,256]{3,0,2,1:T(1,128)} %param.15) | copy-start | bytes 414724
  4.2 0.9 %copy-start = (f32[6,27,27]{2,1,0:T(8,128)S(1)}, f32[6,27,27]{2,1,0:T(8,128)}, u32[]{:S(2)}) copy-start(f32[6,27,27]{2,1,0:T(8,128)} %lift.1) | copy-start | bytes 52492
  4.2 0.9 %copy-start.1 = (f32[27,27]{1,0:T(8,128)S(1)}, f32[27,27]{1,0:T(8,128)}, u32[]{:S(2)}) copy-start(f32[27,27]{1,0:T(8,128)} %smooth.1) | copy-start | bytes 8752
  4.2 0.9 %copy-start.2 = (f32[27,27]{1,0:T(8,128)S(1)}, f32[27,27]{1,0:T(8,128)}, u32[]{:S(2)}) copy-start(f32[27,27]{1,0:T(8,128)} %stiff.1) | copy-start | bytes 8752
  4.2 0.9 %copy-start.3 = (f32[27,27]{1,0:T(8,128)S(1)}, f32[27,27]{1,0:T(8,128)}, u32[]{:S(2)}) copy-start(f32[27,27]{1,0:T(8,128)} %mass_inv.1) | copy-start | bytes 8752
  4.3 0.9 %copy-start.4 = (f32[6,3,27]{2,1,0:T(4,128)S(1)}, f32[6,3,27]{2,1,0:T(4,128)}, u32[]{:S(2)}) copy-start(f32[6,3,27]{2,1,0:T(4,128)} %face_geo.1) | copy-start | bytes 5836
  4.3 0.9 %copy-start.5 = (s32[1,4,32]{2,1,0:T(4,128)S(1)}, s32[1,4,32]{2,1,0:T(4,128)}, u32[]{:S(2)}) copy-start(s32[1,4,32]{2,1,0:T(4,128)} %send_nodes.1) | copy-start | bytes 1540
  4.3 0.9 %copy-start.6 = (s32[1,4,32]{2,1,0:T(4,128)S(1)}, s32[1,4,32]{2,1,0:T(4,128)}, u32[]{:S(2)}) copy-start(s32[1,4,32]{2,1,0:T(4,128)} %recv_nodes.1) | copy-start | bytes 1540
  4.3 0.9 %copy-start.7 = (s32[1,4,16]{2,1,0:T(4,128)S(1)}, s32[1,4,16]{2,1,0:T(4,128)}, u32[]{:S(2)}) copy-start(s32[1,4,16]{2,1,0:T(4,128)} %send_elems.1) | copy-start | bytes 772

commit v2 on v1

--- a/solution.py
+++ b/solution.py
@@ -16,7 +16,7 @@
 MESH = pl.DeviceIdType.MESH
 LANES = 128
 ROWS = 32
-RADIX = 32
+RADIX = 4
 
 
 def rounds_of(parts):
@@ -69,9 +69,9 @@
     vs_sem, vr_sem, gs_sem, gr_sem, ms_sem, mr_sem,
 ):
     me = lax.axis_index("dom")
-    basis, elems = conn.shape[1], conn.shape[2]
-    fields = states.shape[1]
-    faces = neighbours.shape[1]
+    basis, elems = conn.shape[0], conn.shape[2]
+    fields = states.shape[0]
+    faces = neighbours.shape[0]
     nodes = pos.shape[2]
     groups = nodes // LANES
     halves = elems // LANES
@@ -94,7 +94,7 @@
 
     u_ref[...] = jnp.zeros(u_ref.shape, F32)
     for v in range(fields):
-        u_ref[v * ROWS : v * ROWS + basis, :] = states[0, v]
+        u_ref[v * ROWS : v * ROWS + basis, :] = states[v, :, 0, :]
 
     lane = iota((8, LANES), 1)
     row = iota((8, LANES), 0)
@@ -155,15 +155,15 @@
     for c in range(3):
         for g in range(groups):
             r = c * groups + g
-            x0_ref[r : r + 1, :] = pos[0, c : c + 1, g * LANES : (g + 1) * LANES]
+            x0_ref[r : r + 1, :] = pos[c, 0:1, g * LANES : (g + 1) * LANES]
     x_ref[...] = x0_ref[...]
     s_ref[...] = jnp.zeros(s_ref.shape, F32)
 
     alive = (iota((1, elems), 1) < live[0])
     lo_ref[...] = jnp.zeros(lo_ref.shape, jnp.int32)
     hi_ref[...] = jnp.zeros(hi_ref.shape, jnp.int32)
-    lo_ref[0:basis, :] = conn[0] & (LANES - 1)
-    hi_ref[0:basis, :] = conn[0] >> 7
+    lo_ref[0:basis, :] = conn[:, 0, :] & (LANES - 1)
+    hi_ref[0:basis, :] = conn[:, 0, :] >> 7
 
     sub_lo = iota((LANES, elems), 0)
     sub_hi = iota((groups, elems), 0)
@@ -274,14 +274,14 @@
     for c in range(3):
         for g in range(groups):
             r = c * groups + g
-            out_c[0, c : c + 1, g * LANES : (g + 1) * LANES] = x_ref[r : r + 1, :]
+            out_c[c, 0:1, g * LANES : (g + 1) * LANES] = x_ref[r : r + 1, :]
 
     x_ref[...] = x_ref[...] - x0_ref[...]
     near = corners(x_ref)
     projected = jnp.zeros((8, elems), F32)
     for c in range(3):
         projected = projected + mm3(split(fg_ref[c * 8 : c * 8 + 8, 0:ROWS]), near[c])
-    rate = rates[0] * (1.0 + 0.5 * jnp.tanh(projected[0:faces])) * jnp.where(alive, 1.0, 0.0)
+    rate = rates[:, 0, :] * (1.0 + 0.5 * jnp.tanh(projected[0:faces])) * jnp.where(alive, 1.0, 0.0)
     rate_ref[0:faces, :] = rate
     most = jnp.max(jnp.sum(rate, axis=0, keepdims=True), axis=1, keepdims=True)
     m_send[0] = jnp.broadcast_to(most, (8, LANES))
@@ -293,7 +293,7 @@
             for h in range(halves):
                 for f in range(faces):
                     which = jnp.broadcast_to(
-                        neighbours[0, f : f + 1, h * LANES : (h + 1) * LANES], (ROWS, LANES)
+                        neighbours[f, 0:1, h * LANES : (h + 1) * LANES], (ROWS, LANES)
                     )
                     low, far = which & (LANES - 1), which >> 7
                     got = pick(u_ref[v * ROWS : (v + 1) * ROWS, 0:LANES], low)
@@ -314,7 +314,7 @@
             r = (v * faces + f) * ROWS
             for h in range(halves):
                 which = jnp.broadcast_to(
-                    neighbours[0, f : f + 1, h * LANES : (h + 1) * LANES], (ROWS, LANES)
+                    neighbours[f, 0:1, h * LANES : (h + 1) * LANES], (ROWS, LANES)
                 )
                 got = pick(ghost, (which + ghosts * v) & (LANES - 1))
                 cols.append(jnp.where(which >= elems, got, nb_ref[r : r + ROWS, h * LANES : (h + 1) * LANES]))
@@ -352,7 +352,7 @@
             if step < STEPS - 1:
                 u_ref[v * ROWS : (v + 1) * ROWS, :] = new
             else:
-                out_u[0, v] = new[0:basis, :]
+                out_u[v, :, 0, :] = new[0:basis, :]
 
     for sweep in range(SWEEPS):
         for k in range(4):
@@ -408,11 +408,15 @@
         pltpu.SemaphoreType.DMA((max(total, 1),)),
         pltpu.SemaphoreType.DMA((max(total, 1),)),
     ]
-    return pl.pallas_call(
+    rowed = [
+        a.reshape(a.shape[1:-1] + (1, a.shape[-1])) if i in (0, 1, 2, 6, 10) else a
+        for i, a in enumerate(args)
+    ]
+    new_c, new_u = pl.pallas_call(
         functools.partial(kernel, parts, shifts, rounds),
         out_shape=(
-            jax.ShapeDtypeStruct(pos.shape, F32),
-            jax.ShapeDtypeStruct(states.shape, F32),
+            jax.ShapeDtypeStruct(rowed[0].shape, F32),
+            jax.ShapeDtypeStruct(rowed[1].shape, F32),
         ),
         in_specs=specs,
         out_specs=(vmem, vmem),
@@ -420,7 +424,8 @@
         compiler_params=pltpu.CompilerParams(
             collective_id=0, has_side_effects=True, vmem_limit_bytes=32 * 1024 * 1024
         ),
-    )(*args)
+    )(*rowed)
+    return new_c.reshape(pos.shape), new_u.reshape(states.shape)
 
 
 def solution(mesh):

time: 55.5 us -> 62.6 us (1.13)
  local copies, waits for them, and re-layouts: 5.17 us -> 9.46 us
  Pallas kernels: 48.5 us -> 51.1 us
    unnamed x23 -> x28, local copies, waits for them, and re-layouts: 3.74 us -> 9.46 us
    pallas_call x1, Pallas kernels: 48.5 us -> 51.1 us  [on_device(): pl.pallas_call(functools.partial(kernel, parts, shifts, rounds), out_shap...]
    pallas_call x2 -> x0, local copies, waits for them, and re-layouts: 1.43 us -> none  [on_device(): pl.pallas_call(functools.partial(kernel, parts, shifts, rounds), out_shap...]
where the time goes in v2:
time: 62.6 us; the launch traced here: 61.9 us
  Pallas kernels  51.1 us (82%)
  local copies, waits for them, and re-layouts  9.46 us (15%)
  between operations  1.34 us (2%)
    pallas_call x1, Pallas kernels, on_device(): pl.pallas_call(functools.partial(kernel, parts, shifts, rounds), out_shap...  51.1 us
    unnamed x28, local copies, waits for them, and re-layouts  9.46 us

profile of v2, /device:TPU:0, one launch (start us, length us, event | category | flops | bytes accessed | tf_op | source)
XLA Modules:
  0.0 61.9 jit_solution(14845618952243550670)
XLA Ops:
  0.6 0.0 copy-start.8
  1.3 0.0 copy-start.11
  1.3 0.0 copy-start.10
  1.3 0.0 copy-done.8
  1.3 0.7 %copy-done.11 = s32[1,4,32]{2,1,0:T(4,128)S(1)} copy-done((s32[1,4,32]{2,1,0:T(4,128)S(1)}, s32[1,4,32]{2,1,0:T(4,128)}, u32[]{:S(2)}) %copy-start.11) | copy-done | bytes 536
  2.0 0.0 copy-done.10
  2.0 0.0 copy-start
  2.0 0.9 %copy-done = f32[1,5,27,256]{3,0,2,1:T(1,128)S(1)} copy-done((f32[1,5,27,256]{3,0,2,1:T(1,128)S(1)}, f32[1,5,27,256]{3,0,2,1:T(1,128)}, u32[]{:S(2)}) %copy-start) | copy-done | bytes 138264
  2.9 0.0 copy-start.1
  2.9 0.9 %copy-done.1 = f32[6,27,27]{2,1,0:T(8,128)S(1)} copy-done((f32[6,27,27]{2,1,0:T(8,128)S(1)}, f32[6,27,27]{2,1,0:T(8,128)}, u32[]{:S(2)}) %copy-start.1) | copy-done | bytes 17520
  3.8 0.0 copy-start.2
  3.8 0.7 %copy-done.2 = s32[1,27,256]{2,0,1:T(1,128)S(1)} copy-done((s32[1,27,256]{2,0,1:T(1,128)S(1)}, s32[1,27,256]{2,0,1:T(1,128)}, u32[]{:S(2)}) %copy-start.2) | copy-done | bytes 27672
  4.5 0.0 copy-start.3
  4.6 0.7 %copy-done.3 = f32[1,3,2048]{2,0,1:T(1,128)S(1)} copy-done((f32[1,3,2048]{2,0,1:T(1,128)S(1)}, f32[1,3,2048]{2,0,1:T(1,128)}, u32[]{:S(2)}) %copy-start.3) | copy-done | bytes 24600
  5.3 0.0 copy-start.4
  5.3 0.7 %copy-done.4 = f32[27,27]{1,0:T(8,128)S(1)} copy-done((f32[27,27]{1,0:T(8,128)S(1)}, f32[27,27]{1,0:T(8,128)}, u32[]{:S(2)}) %copy-start.4) | copy-done | bytes 2940
  6.0 0.7 %copy-done.5 = f32[27,27]{1,0:T(8,128)S(1)} copy-done((f32[27,27]{1,0:T(8,128)S(1)}, f32[27,27]{1,0:T(8,128)}, u32[]{:S(2)}) %copy-start.5) | copy-done | bytes 2940
  6.7 0.7 %copy-done.6 = f32[27,27]{1,0:T(8,128)S(1)} copy-done((f32[27,27]{1,0:T(8,128)S(1)}, f32[27,27]{1,0:T(8,128)}, u32[]{:S(2)}) %copy-start.6) | copy-done | bytes 2940
  7.4 0.7 %copy-done.7 = f32[6,3,27]{2,1,0:T(4,128)S(1)} copy-done((f32[6,3,27]{2,1,0:T(4,128)S(1)}, f32[6,3,27]{2,1,0:T(4,128)}, u32[]{:S(2)}) %copy-start.7) | copy-done | bytes 1968
  8.2 0.7 %copy-done.9 = f32[1,6,256]{2,0,1:T(1,128)S(1)} copy-done((f32[1,6,256]{2,0,1:T(1,128)S(1)}, f32[1,6,256]{2,0,1:T(1,128)}, u32[]{:S(2)}) %copy-start.9) | copy-done | bytes 6168
  8.8 0.7 %copy-done.12 = s32[1,4,16]{2,1,0:T(4,128)S(1)} copy-done((s32[1,4,16]{2,1,0:T(4,128)S(1)}, s32[1,4,16]{2,1,0:T(4,128)}, u32[]{:S(2)}) %copy-start.12) | copy-done | bytes 280
  9.5 51.1 %shard_map.149 = (f32[3,1,2048]{2,1,0:T(1,128)S(1)}, f32[5,27,1,256]{3,2,1,0:T(1,128)S(1)}) custom-call(f32[3,1,2048]{2,1,0:T(1,128)S(1)} %bitcast.10, f32[5,27,1,256]{3,2,1,0:T(1,128)S(1)} %bitcast.7, s32[27,1,256]{2,1,0:T(1,128)S(1)} %bitcast.9, s32[1,4,32]{2,1,0:T(4,128)S(1)} %copy-done.10, s32[1,4,32]{2,1,0:T(4,128)S(1)} %copy-done.11, ...), custom_call_target="tpu_custom_call" | custom-call | tf_op jit(solution)/shard_map/pallas_call | solution.py:415
  60.6 0.6 copy.19
  61.2 0.7 %copy.20 = f32[1,5,27,256]{3,0,2,1:T(1,128)} copy(f32[1,5,27,256]{3,0,2,1:T(1,128)S(1)} %bitcast.8) | data formatting | bytes 276480
  (5 shorter events, 0.0 us)
Async XLA Ops:
  0.6 0.7 %copy-start.8 = (s32[1,6,256]{2,0,1:T(1,128)S(1)}, s32[1,6,256]{2,0,1:T(1,128)}, u32[]{:S(2)}) copy-start(s32[1,6,256]{2,0,1:T(1,128)} %param.20) | copy-start | bytes 18436
  1.3 0.7 %copy-start.11 = (s32[1,4,32]{2,1,0:T(4,128)S(1)}, s32[1,4,32]{2,1,0:T(4,128)}, u32[]{:S(2)}) copy-start(s32[1,4,32]{2,1,0:T(4,128)} %recv_nodes.1) | copy-start | bytes 1540
  1.3 0.7 %copy-start.10 = (s32[1,4,32]{2,1,0:T(4,128)S(1)}, s32[1,4,32]{2,1,0:T(4,128)}, u32[]{:S(2)}) copy-start(s32[1,4,32]{2,1,0:T(4,128)} %send_nodes.1) | copy-start | bytes 1540
  2.0 0.9 %copy-start = (f32[1,5,27,256]{3,0,2,1:T(1,128)S(1)}, f32[1,5,27,256]{3,0,2,1:T(1,128)}, u32[]{:S(2)}) copy-start(f32[1,5,27,256]{3,0,2,1:T(1,128)} %param.15) | copy-start | bytes 414724
  2.9 0.9 %copy-start.1 = (f32[6,27,27]{2,1,0:T(8,128)S(1)}, f32[6,27,27]{2,1,0:T(8,128)}, u32[]{:S(2)}) copy-start(f32[6,27,27]{2,1,0:T(8,128)} %lift.1) | copy-start | bytes 52492
  3.8 0.7 %copy-start.2 = (s32[1,27,256]{2,0,1:T(1,128)S(1)}, s32[1,27,256]{2,0,1:T(1,128)}, u32[]{:S(2)}) copy-start(s32[1,27,256]{2,0,1:T(1,128)} %param.16) | copy-start | bytes 82948
  4.5 0.7 %copy-start.3 = (f32[1,3,2048]{2,0,1:T(1,128)S(1)}, f32[1,3,2048]{2,0,1:T(1,128)}, u32[]{:S(2)}) copy-start(f32[1,3,2048]{2,0,1:T(1,128)} %param.14) | copy-start | bytes 73732
  5.3 0.7 %copy-start.4 = (f32[27,27]{1,0:T(8,128)S(1)}, f32[27,27]{1,0:T(8,128)}, u32[]{:S(2)}) copy-start(f32[27,27]{1,0:T(8,128)} %smooth.1) | copy-start | bytes 8752
  6.0 0.7 %copy-start.5 = (f32[27,27]{1,0:T(8,128)S(1)}, f32[27,27]{1,0:T(8,128)}, u32[]{:S(2)}) copy-start(f32[27,27]{1,0:T(8,128)} %stiff.1) | copy-start | bytes 8752
  6.7 0.7 %copy-start.6 = (f32[27,27]{1,0:T(8,128)S(1)}, f32[27,27]{1,0:T(8,128)}, u32[]{:S(2)}) copy-start(f32[27,27]{1,0:T(8,128)} %mass_inv.1) | copy-start | bytes 8752
  7.4 0.7 %copy-start.7 = (f32[6,3,27]{2,1,0:T(4,128)S(1)}, f32[6,3,27]{2,1,0:T(4,128)}, u32[]{:S(2)}) copy-start(f32[6,3,27]{2,1,0:T(4,128)} %face_geo.1) | copy-start | bytes 5836
  8.1 0.7 %copy-start.9 = (f32[1,6,256]{2,0,1:T(1,128)S(1)}, f32[1,6,256]{2,0,1:T(1,128)}, u32[]{:S(2)}) copy-start(f32[1,6,256]{2,0,1:T(1,128)} %param.24) | copy-start | bytes 18436
  8.8 0.7 %copy-start.12 = (s32[1,4,16]{2,1,0:T(4,128)S(1)}, s32[1,4,16]{2,1,0:T(4,128)}, u32[]{:S(2)}) copy-start(s32[1,4,16]{2,1,0:T(4,128)} %send_elems.1) | copy-start | bytes 772
